TPU v7x, 256 devices: a whole 4x4x8 slice. The times are simulated.
256 devices in a mesh: lat: 8 (over x_hi, y), lon: 32 (over x_lo, z, core).
Axes of the slice: x: 4 (x_hi: 2, x_lo: 2; x = x_hi * 2 + x_lo), y: 4, z: 8, core: 2. Of those that a mesh axis runs over, the one named last changes fastest.
Arguments:
- inputs: bfloat16 [720, 1440, 256], P('lat', 'lon'), may hold values from -6 to 6
- kernel: bfloat16 [3, 3, 256, 256], replicated, may hold values from -0.125 to 0.125
- cotangent: bfloat16 [720, 1440, 256], P('lat', 'lon'), may hold values from -6 to 6
Outputs:
- outputs: bfloat16 [720, 1440, 256], P('lat', 'lon')
- input_grad: bfloat16 [720, 1440, 256], P('lat', 'lon')
- kernel_grad: float32 [3, 3, 256, 256], replicated
All inputs are finite; a program needn't handle non-finite values.
Results may differ from a plain program's by a relative error of at most 0.001.
Values may be sent and summed in bfloat16 or wider, within the bound.
A program may use at most 192 MiB of HBM per device.

v0:
```python
import math
import jax
import jax.numpy as jnp
from jax import lax
from jax.sharding import PartitionSpec as P


def with_halo(cells, sides, width):
    for axis, dim in sides:
        count = lax.axis_size(axis)
        head = lax.slice_in_dim(cells, 0, width, axis=dim)
        tail = lax.slice_in_dim(cells, cells.shape[dim] - width, cells.shape[dim], axis=dim)
        cells = jnp.concatenate(
            [
                lax.ppermute(tail, axis, [(i, (i + 1) % count) for i in range(count)]),
                cells,
                lax.ppermute(head, axis, [((i + 1) % count, i) for i in range(count)]),
            ],
            axis=dim,
        )
    return cells


def from_behind(value, axis, steps):
    count = lax.axis_size(axis)
    pairs = [(source, (source + steps) % count) for source in range(count)]
    return lax.ppermute(value, axis, pairs)


def patches(padded, rows, cols):
    pieces = [
        padded[row_tap : row_tap + rows, col_tap : col_tap + cols]
        for row_tap in range(3)
        for col_tap in range(3)
    ]
    return jnp.concatenate(pieces, axis=-1).reshape(rows * cols, -1)


def surround(field):
    return with_halo(field, (("lat", 0), ("lon", 1)), 1)


def polar(padded):
    both = jnp.stack([padded[1], padded[-2]])
    moved = from_behind(both, "lon", lax.axis_size("lon") // 2)
    return (moved[0], moved[1])


def edge_term(row_data, weights, cols, width):
    stacked = jnp.concatenate([row_data[offset : offset + cols] for offset in range(3)], axis=-1)
    return jnp.dot(stacked, weights.reshape(-1, width), preferred_element_type=jnp.float32)


def local(inputs, kernel, cotangent):
    rows, cols, width = inputs.shape
    north = lax.axis_index("lat") == 0
    south = lax.axis_index("lat") == lax.axis_size("lat") - 1
    padded = surround(inputs)
    top, bottom = polar(padded)
    padded = jnp.concatenate(
        [
            jnp.where(north, top, padded[0])[None],
            padded[1:-1],
            jnp.where(south, bottom, padded[-1])[None],
        ],
        0,
    )
    columns = patches(padded, rows, cols)
    outputs = jnp.dot(columns, kernel.reshape(-1, width), preferred_element_type=jnp.float32)
    outputs = outputs.reshape(rows, cols, width).astype(jnp.bfloat16)
    flat_grad = cotangent.reshape(-1, width)
    local_grad = lax.dot_general(
        columns, flat_grad, (((0,), (0,)), ((), ())), preferred_element_type=jnp.float32
    )
    local_grad = local_grad.reshape(3, 3, width, width)
    padded_grad = surround(cotangent)
    grad_top, grad_bottom = polar(padded_grad)
    empty_row = jnp.zeros_like(padded_grad[0])
    padded_grad = jnp.concatenate(
        [
            jnp.where(north, empty_row, padded_grad[0])[None],
            padded_grad[1:-1],
            jnp.where(south, empty_row, padded_grad[-1])[None],
        ],
        0,
    )
    flipped = jnp.transpose(kernel[::-1, ::-1], (0, 1, 3, 2))
    input_grad = jnp.dot(
        patches(padded_grad, rows, cols),
        flipped.reshape(-1, width),
        preferred_element_type=jnp.float32,
    )
    input_grad = input_grad.reshape(rows, cols, width)
    north_term = edge_term(grad_top, flipped[2], cols, width)
    south_term = edge_term(grad_bottom, flipped[0], cols, width)
    input_grad = input_grad.at[0].add(jnp.where(north, north_term, 0.0))
    input_grad = input_grad.at[-1].add(jnp.where(south, south_term, 0.0))
    factor = 1.0 / math.sqrt(rows * cols * lax.axis_size("lat") * lax.axis_size("lon"))
    summed = lax.psum(local_grad, ("lat", "lon"))
    return (outputs, input_grad.astype(jnp.bfloat16), summed * factor)


def solution(mesh):
    in_specs = (P("lat", "lon", None), P(), P("lat", "lon", None))
    out_specs = (P("lat", "lon", None), P("lat", "lon", None), P())
    return jax.shard_map(local, mesh=mesh, in_specs=in_specs, out_specs=out_specs, check_vma=False)
```

profile of v0, /device:TPU:2, one launch (start us, length us, event | category | flops | bytes accessed | tf_op | source)
XLA Modules:
  0.0 427.5 jit_solution(5525735376347575952)
XLA Ops:
  8.0 4.6 %collective-permute-start.1 = (bf16[1,45,256]{2,1,0:T(8,128)(2,1)S(1)}, bf16[1,45,256]{2,1,0:T(8,128)(2,1)S(1)}, u32[]{:S(2)}, u32[]{:S(2)}) collective-permute-start(bf16[1,45,256]{2,1,0:T(8,128)(2,1)S(1)} %get-tuple-element.37), channel_id=1, source_target_pairs={{32,0},{64,32},{96,64},{128,96},{160,128},{192,160},{224,192},{0,2... | collective-permute-start | bytes 69128 | tf_op jit(solution)/shard_map/ppermute | solution.py:17
  13.9 5.6 %collective-permute-start.6 = (bf16[1,45,256]{2,1,0:T(8,128)(2,1)}, bf16[1,45,256]{2,1,0:T(8,128)(2,1)S(1)}, u32[]{:S(2)}, u32[]{:S(2)}) collective-permute-start(bf16[1,45,256]{2,1,0:T(8,128)(2,1)} %get-tuple-element.35), channel_id=1, source_target_pairs={{32,0},{64,32},{96,64},{128,96},{160,128},{192,160},{224,192},{0,2... | collective-permute-start | bytes 69128 | tf_op jit(solution)/shard_map/ppermute | solution.py:17
  23.3 1.9 reshape.103
  25.2 2.0 collective-permute-done.5
  27.6 4.3 collective-permute-start.8
  32.3 3.8 collective-permute-start.3
  38.5 1.7 collective-permute-start.4
  41.9 1.6 fusion.7
  43.5 2.9 fusion.5
  46.3 2.9 fusion.19
  49.3 2.8 fusion.18
  52.0 1.6 constant_dynamic-update-slice_fusion.7
  53.7 3.1 fusion.17
  56.7 1.7 fusion.3
  58.4 2.9 fusion.1
  61.3 2.9 fusion.16
  64.1 9.8 %fusion.72 = f32[90,45,256]{2,1,0:T(8,128)S(1)} fusion(bf16[90,45,2304]{2,1,0:T(8,128)(2,1)} %fusion.16, bf16[2304,256,1]{1,0,2:T(8,128)(2,1)S(1)} %bitcast.50), kind=kOutput, calls=%fused_computation.114 | convolution fusion | flops 4777574400 | bytes 23989248 | tf_op jit(solution)/shard_map/dot_general | solution.py:88
  78.6 1.6 fusion.15
  80.3 2.8 fusion.13
  83.1 2.9 fusion.23
  86.0 2.8 fusion.22
  88.8 1.6 constant_dynamic-update-slice_fusion.3
  90.4 3.1 fusion.21
  93.5 1.7 fusion.11
  95.2 2.8 fusion.9
  98.0 2.8 fusion.20
  100.8 19.4 %reshape.99 = bf16[4050,2304]{1,0:T(8,128)(2,1)} reshape(bf16[90,45,2304]{2,1,0:T(8,128)(2,1)} %fusion.20) | data formatting | bytes 37324800 | tf_op jit(solution)/shard_map/reshape | solution.py:36
  120.2 25.0 %copy.7 = bf16[4050,2304]{0,1:T(8,128)(2,1)} copy(bf16[4050,2304]{1,0:T(8,128)(2,1)} %reshape.99) | data formatting | bytes 37324800 | tf_op jit(solution)/shard_map/reshape | solution.py:36
  145.1 10.6 %fusion.24 = f32[3,3,256,256]{3,2,1,0:T(8,128)} fusion(bf16[3,3,256,4050]{3,2,1,0:T(8,128)(2,1)} %bitcast.46, bf16[4050,256,1,1]{1,0,2,3:T(8,128)(2,1)S(1)} %copy-done.2), kind=kOutput, calls=%fused_computation.42 | convolution fusion | flops 4777574400 | bytes 23095296 | tf_op jit(solution)/shard_map/dot_general | solution.py:72
  157.0 11.5 %convolution_convert_fusion = bf16[90,45,256]{2,1,0:T(8,128)(2,1)} fusion(bf16[90,45,2304]{2,1,0:T(8,128)(2,1)} %fusion.20, bf16[2304,256,1]{1,0,2:T(8,128)(2,1)S(1)} %bitcast.49), kind=kOutput, calls=%fused_computation.44 | convolution fusion | flops 4778611200 | bytes 21915648 | tf_op jit(solution)/shard_map/dot_general | solution.py:69
  168.5 248.7 %all-reduce.2.cloned.1.call-done = f32[3,3,256,256]{3,2,1,0:T(8,128)} async-done(((f32[3,3,256,256]{3,2,1,0:T(8,128)}), f32[3,3,256,256]{3,2,1,0:T(8,128)}) %all-reduce.2.cloned.1.call-update) | async-done | bytes 2359312 | tf_op jit(solution)/shard_map/psum | solution.py:99
  417.2 3.3 broadcast_multiply_fusion
  (56 shorter events, 16.5 us)
Async XLA Ops:
  7.2 410.0 %all-reduce.2.cloned.1.call-start = ((), (), s32[]{:S(2)}) async-start(), calls=%async_computation | async-start | bytes 4718592 | tf_op jit(solution)/shard_map/psum | solution.py:99
  8.0 24.1 %collective-permute-start.1 = (bf16[1,45,256]{2,1,0:T(8,128)(2,1)S(1)}, bf16[1,45,256]{2,1,0:T(8,128)(2,1)S(1)}, u32[]{:S(2)}, u32[]{:S(2)}) collective-permute-start(bf16[1,45,256]{2,1,0:T(8,128)(2,1)S(1)} %get-tuple-element.37), channel_id=1, source_target_pairs={{32,0},{64,32},{96,64},{128,96},{160,128},{192,160},{224,192},{0,2... | collective-permute-start | bytes 69128 | tf_op jit(solution)/shard_map/ppermute | solution.py:17
  12.5 19.3 %collective-permute-start = (bf16[1,45,256]{2,1,0:T(8,128)(2,1)S(1)}, bf16[1,45,256]{2,1,0:T(8,128)(2,1)S(1)}, u32[]{:S(2)}, u32[]{:S(2)}) collective-permute-start(bf16[1,45,256]{2,1,0:T(8,128)(2,1)S(1)} %get-tuple-element.38), channel_id=1, source_target_pairs={{0,32},{32,64},{64,96},{96,128},{128,160},{160,192},{192,224},{224... | collective-permute-start | bytes 69128 | tf_op jit(solution)/shard_map/ppermute | solution.py:15
  13.9 13.4 %collective-permute-start.6 = (bf16[1,45,256]{2,1,0:T(8,128)(2,1)}, bf16[1,45,256]{2,1,0:T(8,128)(2,1)S(1)}, u32[]{:S(2)}, u32[]{:S(2)}) collective-permute-start(bf16[1,45,256]{2,1,0:T(8,128)(2,1)} %get-tuple-element.35), channel_id=1, source_target_pairs={{32,0},{64,32},{96,64},{128,96},{160,128},{192,160},{224,192},{0,2... | collective-permute-start | bytes 69128 | tf_op jit(solution)/shard_map/ppermute | solution.py:17
  19.6 7.7 %collective-permute-start.5 = (bf16[1,45,256]{2,1,0:T(8,128)(2,1)}, bf16[1,45,256]{2,1,0:T(8,128)(2,1)S(1)}, u32[]{:S(2)}, u32[]{:S(2)}) collective-permute-start(bf16[1,45,256]{2,1,0:T(8,128)(2,1)} %get-tuple-element.36), channel_id=1, source_target_pairs={{0,32},{32,64},{64,96},{96,128},{128,160},{160,192},{192,224},{224... | collective-permute-start | bytes 69128 | tf_op jit(solution)/shard_map/ppermute | solution.py:15
  21.2 2.0 copy-start
  27.2 4.7 %copy-start.1 = (bf16[90,45,256]{2,1,0:T(8,128)(2,1)S(1)}, bf16[90,45,256]{2,1,0:T(8,128)(2,1)}, u32[]{:S(2)}) copy-start(bf16[90,45,256]{2,1,0:T(8,128)(2,1)} %param.7) | copy-start | bytes 6220804
  27.5 8.6 %collective-permute-start.7 = (bf16[92,1,256]{2,1,0:T(2,128)(2,1)S(1)}, bf16[92,1,256]{2,1,0:T(2,128)(2,1)S(1)}, u32[]{:S(2)}, u32[]{:S(2)}) collective-permute-start(bf16[92,1,256]{2,1,0:T(2,128)(2,1)S(1)} %get-tuple-element.31), channel_id=1, source_target_pairs={{0,1},{1,2},{2,3},{3,4},{4,5},{5,6},{6,7},{7,8},{8,9},{9,10},{10,1... | collective-permute-start | bytes 141320 | tf_op jit(solution)/shard_map/ppermute | solution.py:15
  27.6 8.5 %collective-permute-start.8 = (bf16[92,1,256]{2,1,0:T(2,128)(2,1)S(1)}, bf16[92,1,256]{2,1,0:T(2,128)(2,1)S(1)}, u32[]{:S(2)}, u32[]{:S(2)}) collective-permute-start(bf16[92,1,256]{2,1,0:T(2,128)(2,1)S(1)} %get-tuple-element.32), channel_id=1, source_target_pairs={{1,0},{2,1},{3,2},{4,3},{5,4},{6,5},{7,6},{8,7},{9,8},{10,9},{11,1... | collective-permute-start | bytes 141320 | tf_op jit(solution)/shard_map/ppermute | solution.py:17
  32.2 6.2 %collective-permute-start.2 = (bf16[92,1,256]{2,1,0:T(2,128)(2,1)S(1)}, bf16[92,1,256]{2,1,0:T(2,128)(2,1)S(1)}, u32[]{:S(2)}, u32[]{:S(2)}) collective-permute-start(bf16[92,1,256]{2,1,0:T(2,128)(2,1)S(1)} %get-tuple-element.33), channel_id=1, source_target_pairs={{0,1},{1,2},{2,3},{3,4},{4,5},{5,6},{6,7},{7,8},{8,9},{9,10},{10,1... | collective-permute-start | bytes 141320 | tf_op jit(solution)/shard_map/ppermute | solution.py:15
  32.3 6.1 %collective-permute-start.3 = (bf16[92,1,256]{2,1,0:T(2,128)(2,1)S(1)}, bf16[92,1,256]{2,1,0:T(2,128)(2,1)S(1)}, u32[]{:S(2)}, u32[]{:S(2)}) collective-permute-start(bf16[92,1,256]{2,1,0:T(2,128)(2,1)S(1)} %get-tuple-element.34), channel_id=1, source_target_pairs={{1,0},{2,1},{3,2},{4,3},{5,4},{6,5},{7,6},{8,7},{9,8},{10,9},{11,1... | collective-permute-start | bytes 141320 | tf_op jit(solution)/shard_map/ppermute | solution.py:17
  36.2 39.5 %collective-permute-start.9 = (bf16[2,47,256]{2,1,0:T(8,128)(2,1)S(1)}, bf16[2,47,256]{2,1,0:T(8,128)(2,1)S(1)}, u32[]{:S(2)}, u32[]{:S(2)}) collective-permute-start(bf16[2,47,256]{2,1,0:T(8,128)(2,1)S(1)} %fusion.57), channel_id=1, source_target_pairs={{0,16},{1,17},{2,18},{3,19},{4,20},{5,21},{6,22},{7,23},{8,24},{9,... | collective-permute-start | bytes 144392 | tf_op jit(solution)/shard_map/ppermute | solution.py:27
  38.5 40.2 %collective-permute-start.4 = (bf16[2,47,256]{2,1,0:T(8,128)(2,1)S(1)}, bf16[2,47,256]{2,1,0:T(8,128)(2,1)S(1)}, u32[]{:S(2)}, u32[]{:S(2)}) collective-permute-start(bf16[2,47,256]{2,1,0:T(8,128)(2,1)S(1)} %fusion.54), channel_id=1, source_target_pairs={{0,16},{1,17},{2,18},{3,19},{4,20},{5,21},{6,22},{7,23},{8,24},{9,... | collective-permute-start | bytes 144392 | tf_op jit(solution)/shard_map/ppermute | solution.py:27
  61.3 2.9 copy-start.6
  75.6 1.0 copy-start.4
  75.6 1.2 copy-start.3
  120.2 25.0 %copy-start.2 = (bf16[4050,256,1,1]{1,0,2,3:T(8,128)(2,1)S(1)}, bf16[4050,256,1,1]{1,0,2,3:T(8,128)(2,1)}, u32[]{:S(2)}) copy-start(bf16[4050,256,1,1]{1,0,2,3:T(8,128)(2,1)} %reshape.103) | copy-start | bytes 6220804
  155.7 1.3 copy-start.5
Sparse Core Ops, SparseCore 0:
  155.9 261.2 all-reduce.1
where the time goes:
time: 435 us; the launch traced here: 428 us
  waiting for transfers between devices  252 us (58%)
  local copies, waits for them, and re-layouts  58.2 us (13%)
  other arithmetic  49.3 us (11%)
  matrix products  32.3 us (7%)
  starting transfers between devices  21.3 us (5%)
  between operations  14.5 us (3%)
    psum x1, waiting for transfers between devices, local(): summed = lax.psum(local_grad, ('lat', 'lon'))  249 us
    reshape x2, local copies, waits for them, and re-layouts, patches(): return jnp.concatenate(pieces, axis=-1).reshape(rows * cols, -1)  44.3 us
    unnamed x14, other arithmetic  35.5 us
    ppermute x4, starting transfers between devices, with_halo(): lax.ppermute(head, axis, [((i + 1) % count, i) for i in range(count)])  18.3 us
    dot_general x1, matrix products, local(): jnp.dot(columns, kernel.reshape(-1, width), preferred_element_type=jnp.fl...  11.5 us
    dot_general x1, matrix products, local(): lax.dot_general(columns, flat_grad, (((0,), (0,)), ((), ())), preferred_e...  10.6 us
    dot_general x1, matrix products, local(): jnp.dot(patches(padded_grad, rows, cols), flipped.reshape(-1, width), pre...  9.85 us
  transfers between devices with their start and end apart: 11, of which 3 were waited for; matrix products, arithmetic and copies ran while one was open for 13% of the time, Pallas kernels for 0%

commit v1 on v0

--- a/solution.py
+++ b/solution.py
@@ -96,7 +96,9 @@
     input_grad = input_grad.at[0].add(jnp.where(north, north_term, 0.0))
     input_grad = input_grad.at[-1].add(jnp.where(south, south_term, 0.0))
     factor = 1.0 / math.sqrt(rows * cols * lax.axis_size("lat") * lax.axis_size("lon"))
-    summed = lax.psum(local_grad, ("lat", "lon"))
+    summed = local_grad
+    for mesh_axis in ("lon", "lat"):
+        summed = lax.psum(summed, mesh_axis)
     return (outputs, input_grad.astype(jnp.bfloat16), summed * factor)
 
 

time: 435 us -> 464 us (1.067)
  waiting for transfers between devices: 252 us -> 275 us
    psum x1 -> x2, waiting for transfers between devices: 249 us -> 271 us  [local(): summed = lax.psum(summed, mesh_axis)]
  transfers between devices with their start and end apart: 11 -> 12, of which waited for: 3 -> 5; matrix products, arithmetic and copies ran while one was open for 13% -> 14% of each run, Pallas kernels for 0% -> 0%
where the time goes in v1:
time: 464 us; the launch traced here: 458 us
  waiting for transfers between devices  275 us (59%)
  local copies, waits for them, and re-layouts  62.3 us (13%)
  other arithmetic  52.2 us (11%)
  matrix products  32.4 us (7%)
  starting transfers between devices  20.7 us (4%)
  between operations  14.5 us (3%)
    psum x2, waiting for transfers between devices, local(): summed = lax.psum(summed, mesh_axis)  271 us
    reshape x2, local copies, waits for them, and re-layouts, patches(): return jnp.concatenate(pieces, axis=-1).reshape(rows * cols, -1)  44.2 us
    unnamed x14, other arithmetic  35.8 us
    ppermute x4, starting transfers between devices, with_halo(): lax.ppermute(head, axis, [((i + 1) % count, i) for i in range(count)])  18.9 us
    dot_general x1, matrix products, local(): jnp.dot(columns, kernel.reshape(-1, width), preferred_element_type=jnp.fl...  11.6 us
    dot_general x1, matrix products, local(): lax.dot_general(columns, flat_grad, (((0,), (0,)), ((), ())), preferred_e...  10.6 us
    dot_general x1, matrix products, local(): jnp.dot(patches(padded_grad, rows, cols), flipped.reshape(-1, width), pre...  9.83 us
  transfers between devices with their start and end apart: 12, of which 5 were waited for; matrix products, arithmetic and copies ran while one was open for 14% of the time, Pallas kernels for 0%

profile of v1, /device:TPU:2, one launch (start us, length us, event | category | flops | bytes accessed | tf_op | source)
XLA Modules:
  0.0 457.6 jit_solution(2365952053338268052)
XLA Ops:
  8.6 4.6 collective-permute-start.1
  14.5 5.6 %collective-permute-start.6 = (bf16[1,45,256]{2,1,0:T(8,128)(2,1)S(1)}, bf16[1,45,256]{2,1,0:T(8,128)(2,1)S(1)}, u32[]{:S(2)}, u32[]{:S(2)}) collective-permute-start(bf16[1,45,256]{2,1,0:T(8,128)(2,1)S(1)} %get-tuple-element.35), channel_id=1, source_target_pairs={{32,0},{64,32},{96,64},{128,96},{160,128},{192,160},{224,192},{0,2... | collective-permute-start | bytes 69128 | tf_op jit(solution)/shard_map/ppermute | solution.py:17
  20.2 1.7 copy.6
  23.0 1.9 reshape.103
  24.9 1.9 constant_dynamic-update-slice_fusion.1
  28.1 4.8 %collective-permute-start.3 = (bf16[92,1,256]{2,1,0:T(2,128)(2,1)S(1)}, bf16[92,1,256]{2,1,0:T(2,128)(2,1)S(1)}, u32[]{:S(2)}, u32[]{:S(2)}) collective-permute-start(bf16[92,1,256]{2,1,0:T(2,128)(2,1)S(1)} %get-tuple-element.34), channel_id=1, source_target_pairs={{1,0},{2,1},{3,2},{4,3},{5,4},{6,5},{7,6},{8,7},{9,8},{10,9},{11,1... | collective-permute-start | bytes 141320 | tf_op jit(solution)/shard_map/ppermute | solution.py:17
  32.9 2.2 collective-permute-done.2
  37.7 1.8 collective-permute-done.4
  41.2 2.8 fusion.13
  44.1 2.8 fusion.23
  46.9 2.9 fusion.22
  51.5 3.0 fusion.21
  54.5 1.7 fusion.11
  56.2 2.9 fusion.9
  59.1 2.7 fusion.20
  61.8 19.9 %reshape.99 = bf16[4050,2304]{1,0:T(8,128)(2,1)} reshape(bf16[90,45,2304]{2,1,0:T(8,128)(2,1)} %fusion.20) | data formatting | bytes 37324800 | tf_op jit(solution)/shard_map/reshape | solution.py:36
  81.7 24.3 %copy.7 = bf16[4050,2304]{0,1:T(8,128)(2,1)} copy(bf16[4050,2304]{1,0:T(8,128)(2,1)} %reshape.99) | data formatting | bytes 37324800 | tf_op jit(solution)/shard_map/reshape | solution.py:36
  106.0 10.6 %fusion.24 = f32[3,3,256,256]{3,2,1,0:T(8,128)} fusion(bf16[3,3,256,4050]{3,2,1,0:T(8,128)(2,1)} %bitcast.46, bf16[4050,256,1,1]{1,0,2,3:T(8,128)(2,1)} %reshape.103), kind=kOutput, calls=%fused_computation.42 | convolution fusion | flops 4777574400 | bytes 23095296 | tf_op jit(solution)/shard_map/dot_general | solution.py:72
  117.5 3.9 collective-permute-start.8
  121.4 2.0 fusion.71
  126.6 2.3 pad_maximum_fusion.1
  131.3 2.7 fusion.5
  134.1 2.8 fusion.19
  136.8 3.6 fusion.18
  142.0 2.9 fusion.17
  146.5 2.7 fusion.1
  149.3 2.8 fusion.16
  152.1 194.2 %all-reduce.3.cloned.1.call-done = f32[3,3,256,256]{3,2,1,0:T(8,128)} async-done(((f32[3,3,256,256]{3,2,1,0:T(8,128)}), f32[3,3,256,256]{3,2,1,0:T(8,128)}) %all-reduce.3.cloned.1.call-update) | async-done | bytes 2359312 | tf_op jit(solution)/shard_map/psum | solution.py:101
  346.3 9.8 %fusion.72 = f32[90,45,256]{2,1,0:T(8,128)S(1)} fusion(bf16[90,45,2304]{2,1,0:T(8,128)(2,1)} %fusion.16, bf16[2304,256,1]{1,0,2:T(8,128)(2,1)S(1)} %bitcast.50), kind=kOutput, calls=%fused_computation.114 | convolution fusion | flops 4777574400 | bytes 23989248 | tf_op jit(solution)/shard_map/dot_general | solution.py:88
  359.1 11.6 %convolution_convert_fusion = bf16[90,45,256]{2,1,0:T(8,128)(2,1)} fusion(bf16[90,45,2304]{2,1,0:T(8,128)(2,1)} %fusion.20, bf16[2304,256,1]{1,0,2:T(8,128)(2,1)S(1)} %bitcast.49), kind=kOutput, calls=%fused_computation.44 | convolution fusion | flops 4778611200 | bytes 21915648 | tf_op jit(solution)/shard_map/dot_general | solution.py:69
  370.7 76.5 %all-reduce.5.cloned.1.call-done = f32[3,3,256,256]{3,2,1,0:T(8,128)} async-done(((f32[3,3,256,256]{3,2,1,0:T(8,128)}), f32[3,3,256,256]{3,2,1,0:T(8,128)}) %all-reduce.5.cloned.1.call-update) | async-done | bytes 2359312 | tf_op jit(solution)/shard_map/psum | solution.py:101
  447.2 3.3 broadcast_multiply_fusion
  (61 shorter events, 23.8 us)
Async XLA Ops:
  7.2 339.1 %all-reduce.3.cloned.1.call-start = ((), (), s32[]{:S(2)}) async-start(), calls=%async_computation | async-start | bytes 4718592 | tf_op jit(solution)/shard_map/psum | solution.py:101
  8.6 18.3 %collective-permute-start.1 = (bf16[1,45,256]{2,1,0:T(8,128)(2,1)S(1)}, bf16[1,45,256]{2,1,0:T(8,128)(2,1)S(1)}, u32[]{:S(2)}, u32[]{:S(2)}) collective-permute-start(bf16[1,45,256]{2,1,0:T(8,128)(2,1)S(1)} %get-tuple-element.37), channel_id=1, source_target_pairs={{32,0},{64,32},{96,64},{128,96},{160,128},{192,160},{224,192},{0,2... | collective-permute-start | bytes 69128 | tf_op jit(solution)/shard_map/ppermute | solution.py:17
  13.2 11.8 %collective-permute-start = (bf16[1,45,256]{2,1,0:T(8,128)(2,1)}, bf16[1,45,256]{2,1,0:T(8,128)(2,1)S(1)}, u32[]{:S(2)}, u32[]{:S(2)}) collective-permute-start(bf16[1,45,256]{2,1,0:T(8,128)(2,1)} %get-tuple-element.38), channel_id=1, source_target_pairs={{0,32},{32,64},{64,96},{96,128},{128,160},{160,192},{192,224},{224... | collective-permute-start | bytes 69128 | tf_op jit(solution)/shard_map/ppermute | solution.py:15
  14.5 18.3 %collective-permute-start.6 = (bf16[1,45,256]{2,1,0:T(8,128)(2,1)S(1)}, bf16[1,45,256]{2,1,0:T(8,128)(2,1)S(1)}, u32[]{:S(2)}, u32[]{:S(2)}) collective-permute-start(bf16[1,45,256]{2,1,0:T(8,128)(2,1)S(1)} %get-tuple-element.35), channel_id=1, source_target_pairs={{32,0},{64,32},{96,64},{128,96},{160,128},{192,160},{224,192},{0,2... | collective-permute-start | bytes 69128 | tf_op jit(solution)/shard_map/ppermute | solution.py:17
  20.2 2.8 copy-start
  20.2 7.7 %collective-permute-start.5 = (bf16[1,45,256]{2,1,0:T(8,128)(2,1)}, bf16[1,45,256]{2,1,0:T(8,128)(2,1)S(1)}, u32[]{:S(2)}, u32[]{:S(2)}) collective-permute-start(bf16[1,45,256]{2,1,0:T(8,128)(2,1)} %get-tuple-element.36), channel_id=1, source_target_pairs={{0,32},{32,64},{64,96},{96,128},{128,160},{160,192},{192,224},{224... | collective-permute-start | bytes 69128 | tf_op jit(solution)/shard_map/ppermute | solution.py:15
  24.9 2.9 copy-start.1
  28.0 7.1 %collective-permute-start.2 = (bf16[92,1,256]{2,1,0:T(2,128)(2,1)S(1)}, bf16[92,1,256]{2,1,0:T(2,128)(2,1)S(1)}, u32[]{:S(2)}, u32[]{:S(2)}) collective-permute-start(bf16[92,1,256]{2,1,0:T(2,128)(2,1)S(1)} %get-tuple-element.33), channel_id=1, source_target_pairs={{0,1},{1,2},{2,3},{3,4},{4,5},{5,6},{6,7},{7,8},{8,9},{9,10},{10,1... | collective-permute-start | bytes 141320 | tf_op jit(solution)/shard_map/ppermute | solution.py:15
  28.1 7.0 %collective-permute-start.3 = (bf16[92,1,256]{2,1,0:T(2,128)(2,1)S(1)}, bf16[92,1,256]{2,1,0:T(2,128)(2,1)S(1)}, u32[]{:S(2)}, u32[]{:S(2)}) collective-permute-start(bf16[92,1,256]{2,1,0:T(2,128)(2,1)S(1)} %get-tuple-element.34), channel_id=1, source_target_pairs={{1,0},{2,1},{3,2},{4,3},{5,4},{6,5},{7,6},{8,7},{9,8},{10,9},{11,1... | collective-permute-start | bytes 141320 | tf_op jit(solution)/shard_map/ppermute | solution.py:17
  35.1 4.5 collective-permute-start.4
  46.9 2.9 copy-start.3
  116.6 330.6 %all-reduce.5.cloned.1.call-start = ((), (), s32[]{:S(2)}) async-start(), calls=%async_computation.1 | async-start | bytes 4718592 | tf_op jit(solution)/shard_map/psum | solution.py:101
  117.5 7.0 %collective-permute-start.7 = (bf16[92,1,256]{2,1,0:T(2,128)(2,1)}, bf16[92,1,256]{2,1,0:T(2,128)(2,1)}, u32[]{:S(2)}, u32[]{:S(2)}) collective-permute-start(bf16[92,1,256]{2,1,0:T(2,128)(2,1)} %get-tuple-element.31), channel_id=1, source_target_pairs={{0,1},{1,2},{2,3},{3,4},{4,5},{5,6},{6,7},{7,8},{8,9},{9,10},{10,1... | collective-permute-start | bytes 141320 | tf_op jit(solution)/shard_map/ppermute | solution.py:15
  117.5 7.0 %collective-permute-start.8 = (bf16[92,1,256]{2,1,0:T(2,128)(2,1)}, bf16[92,1,256]{2,1,0:T(2,128)(2,1)S(1)}, u32[]{:S(2)}, u32[]{:S(2)}) collective-permute-start(bf16[92,1,256]{2,1,0:T(2,128)(2,1)} %get-tuple-element.32), channel_id=1, source_target_pairs={{1,0},{2,1},{3,2},{4,3},{5,4},{6,5},{7,6},{8,7},{9,8},{10,9},{11,1... | collective-permute-start | bytes 141320 | tf_op jit(solution)/shard_map/ppermute | solution.py:17
  125.8 230.3 %collective-permute-start.9 = (bf16[2,47,256]{2,1,0:T(8,128)(2,1)}, bf16[2,47,256]{2,1,0:T(8,128)(2,1)}, u32[]{:S(2)}, u32[]{:S(2)}) collective-permute-start(bf16[2,47,256]{2,1,0:T(8,128)(2,1)} %fusion.57), channel_id=1, source_target_pairs={{0,16},{1,17},{2,18},{3,19},{4,20},{5,21},{6,22},{7,23},{8,24},{9,... | collective-permute-start | bytes 144392 | tf_op jit(solution)/shard_map/ppermute | solution.py:27
  136.8 3.6 copy-start.2
  152.1 194.2 %copy-start.7 = (bf16[3,3,256,256]{2,3,1,0:T(8,128)(2,1)S(1)}, bf16[3,3,256,256]{2,3,1,0:T(8,128)(2,1)}, u32[]{:S(2)}) copy-start(bf16[3,3,256,256]{2,3,1,0:T(8,128)(2,1)} %rev.3) | copy-start | bytes 3538948
  346.3 10.8 %copy-start.5 = (bf16[1,3,256,256]{3,2,1,0:T(8,128)(2,1)S(1)}, bf16[1,3,256,256]{3,2,1,0:T(8,128)(2,1)}, u32[]{:S(2)}) copy-start(bf16[1,3,256,256]{3,2,1,0:T(8,128)(2,1)} %get-tuple-element.40) | copy-start | bytes 1179652
  346.3 11.0 %copy-start.4 = (bf16[1,3,256,256]{3,2,1,0:T(8,128)(2,1)S(1)}, bf16[1,3,256,256]{3,2,1,0:T(8,128)(2,1)}, u32[]{:S(2)}) copy-start(bf16[1,3,256,256]{3,2,1,0:T(8,128)(2,1)} %get-tuple-element.39) | copy-start | bytes 1179652
  357.5 1.6 copy-start.6
Sparse Core Ops, SparseCore 0:
  116.7 229.4 all-reduce.2
  348.9 98.2 all-reduce.4
